TPU v7x, 32 devices: a whole 2x2x4 slice. The times are simulated.
32 devices in a mesh: groups: 2 (over x), ctx: 16 (over z, y, core).
Axes of the slice: x: 2, y: 2, z: 4, core: 2. Of those that a mesh axis runs over, the one named last changes fastest.
Arguments:
- sem_queries: bfloat16 [8192, 1024], P(('groups', 'ctx')), parts along dimension 0, may hold values from -170 to 170
- sem_keys: bfloat16 [8192, 1024], P(('groups', 'ctx')), parts along dimension 0, may hold values from -7 to 7
- sem_values: bfloat16 [8192, 1024], P(('groups', 'ctx')), parts along dimension 0, may hold values from -6 to 6
- sem_inputs: bfloat16 [8192, 2048], P(('groups', 'ctx')), parts along dimension 0, may hold values from -80 to 80
- out_proj: bfloat16 [1024, 2048], P('ctx'), may hold values from -0.5 to 0.5
- norm_gain: float32 [2048], replicated, may hold values from 0.1 to 1.9
- key_proj: bfloat16 [2048, 1024], P('ctx'), may hold values from -0.125 to 0.125
- value_proj: bfloat16 [2048, 1024], P('ctx'), may hold values from -0.125 to 0.125
- slopes: float32 [8], replicated, may hold values from 1 to 16
- coarse_queries: bfloat16 [32768, 1024], P(('groups', 'ctx')), parts along dimension 0, may hold values from -400 to 400
- counts: int32 [32], P(('groups', 'ctx')), parts along dimension 0, may hold values from 512 to 1024, as said below
- band_bounds: int32 [128, 2], P(('groups', 'ctx')), parts along dimension 0, may hold values from 0 to 4096, as said below
Outputs:
- coarse_context: bfloat16 [32768, 1024], P(('groups', 'ctx')), parts along dimension 0
There are 2 independent parts, one for each index of `groups`. A program takes and returns all parts, laid end to end along the dimension named above; an argument that names none is the same for every part. Nothing has to cross between parts.
Inputs may be any that keep to these rules, and one draw needn't show every extreme that they name: `counts`: live coarse tokens of a ctx index fill its first slots; at least half of 1024; some index is full. `band_bounds`: a band of block n, held by ctx index c = n // 4, covers 512 // 2 to 512 rows and lies within the semantic rows of indices c - 1, c and c + 1; block 0 covers exactly 512.
All inputs are finite; a program needn't handle non-finite values.
Results may differ from a plain program's by a relative error of at most 0.0091.
Values may be sent and summed in bfloat16 or wider, within the bound.
A program may use at most 128 MiB of HBM per device.

v0:
```python
import jax
import jax.numpy as jnp
from jax import lax
from jax.sharding import PartitionSpec as P

HEADS = 8
HEAD_DIM = 128
W = 512
BAND = 512
CB = 256


NEG_FILL = -1e30


def passed_along(array, axis, by):
    length = lax.axis_size(axis)
    pairs = [(i, i + by) for i in range(length) if 0 <= i + by < length]
    return lax.ppermute(array, axis, pairs)


def carried_in(array, axis, combine, identity):
    length, position = (lax.axis_size(axis), lax.axis_index(axis))
    everything = lax.all_gather(array, axis)
    start = jnp.broadcast_to(jnp.asarray(identity, array.dtype), array.shape)

    def step(k, before):
        reached = k < position
        new = combine(before, everything[k])
        return jnp.where(reached, new, before)

    return lax.fori_loop(0, length, step, start)


def with_halo(array, sides, width):
    for axis, dim in sides:
        size, length = (lax.axis_size(axis), array.shape[dim])
        up = [(i, (i + 1) % size) for i in range(size - 1)]
        down = [(j, i) for i, j in up]
        last = lax.slice_in_dim(array, length - width, length, axis=dim)
        first = lax.slice_in_dim(array, 0, width, axis=dim)
        before = lax.ppermute(last, axis, up)
        after = lax.ppermute(first, axis, down)
        array = jnp.concatenate([before, array, after], axis=dim)
    return array


def head_split(matrix):
    return matrix.reshape(matrix.shape[0], HEADS, HEAD_DIM)


def attend(queries, key_rows, value_rows, allowed, time_bias):
    scores = jnp.einsum(
        "qhd,khd->hqk",
        head_split(queries),
        head_split(key_rows),
        preferred_element_type=jnp.float32,
    ) * HEAD_DIM ** (-0.5)
    scores = jnp.where(allowed[None], scores + time_bias, NEG_FILL)
    largest = jnp.max(scores, axis=2, keepdims=True)
    exponent = jnp.exp(scores - largest)
    weights = (exponent / jnp.sum(exponent, axis=2, keepdims=True)).astype(jnp.bfloat16)
    blended = jnp.einsum(
        "hqk,khd->qhd", weights, head_split(value_rows), preferred_element_type=jnp.float32
    )
    return blended.reshape(queries.shape[0], -1)


def normalize(sem_stream, norm_gain):
    scaled = sem_stream * lax.rsqrt(
        jnp.mean(sem_stream * sem_stream, axis=1, keepdims=True) + 1e-05
    )
    return (scaled * norm_gain[None, :]).astype(jnp.bfloat16)


def cross_attend(
    queries, key_rows, value_rows, key_global, band_low, band_high, positions, slopes, live_rows
):
    timing = (positions // 2).astype(jnp.float32) * (2.0 / 3.0)
    distance = jnp.abs(timing[:, None] - key_global[None, :].astype(jnp.float32))
    time_bias = -slopes[:, None, None] * distance[None] / BAND
    inside = (key_global >= band_low) & (key_global < band_high)
    allowed = jnp.broadcast_to(inside[None, :], (queries.shape[0], key_global.shape[0]))
    blended = attend(queries, key_rows, value_rows, allowed, time_bias)
    return jnp.where(live_rows[:, None], blended, 0.0).astype(jnp.bfloat16)


def contract_rows(left_side, weight_piece):
    return jnp.dot(left_side, weight_piece, preferred_element_type=jnp.float32)


def add_counts(earlier_sum, later_sum):
    return earlier_sum + later_sum


def on_device(
    sem_queries,
    sem_keys,
    sem_values,
    sem_inputs,
    out_proj,
    norm_gain,
    key_proj,
    value_proj,
    slopes,
    coarse_queries,
    counts,
    band_bounds,
):
    rows_here = sem_queries.shape[0]
    device_index = lax.axis_index("ctx")
    own_pair = jnp.stack([sem_keys, sem_values])
    reach_shards = (W - 1 + rows_here - 1) // rows_here
    earlier = []
    for distance in range(1, reach_shards + 1):
        earlier.insert(0, passed_along(own_pair, "ctx", distance))
    window_pair = jnp.concatenate(earlier + [own_pair], axis=1)
    query_pos = jnp.arange(rows_here, dtype=jnp.int32)
    key_pos = jnp.arange(window_pair.shape[1], dtype=jnp.int32)
    key_lag = query_pos[:, None] + reach_shards * rows_here - key_pos[None, :]
    key_global = device_index * rows_here - reach_shards * rows_here + key_pos
    allowed = (key_lag >= 0) & (key_lag < W) & (key_global[None, :] >= 0)
    sem_att = attend(sem_queries, window_pair[0], window_pair[1], allowed, 0.0).astype(jnp.bfloat16)
    projected = contract_rows(sem_att, lax.all_gather(out_proj, "ctx", axis=0, tiled=True))
    sem_stream = sem_inputs.astype(jnp.float32) + projected
    normed = normalize(sem_stream, norm_gain)
    key_sum = contract_rows(normed, lax.all_gather(key_proj, "ctx", axis=0, tiled=True))
    value_sum = contract_rows(normed, lax.all_gather(value_proj, "ctx", axis=0, tiled=True))
    cross_keys = key_sum.astype(jnp.bfloat16)
    cross_values = value_sum.astype(jnp.bfloat16)
    stream_start = carried_in(counts, "ctx", add_counts, jnp.zeros_like(counts))[0]
    near_pair = with_halo(jnp.stack([cross_keys, cross_values]), (("ctx", 1),), rows_here)
    base_row = (device_index - 1) * rows_here
    live_count = counts[0]
    near_rows = near_pair.shape[1]
    block_total = band_bounds.shape[0]

    def coarse_block(block_index):
        band_low = band_bounds[block_index, 0]
        band_high = band_bounds[block_index, 1]
        first_key = jnp.minimum(band_low - base_row, near_rows - BAND)
        keys_block = lax.dynamic_slice_in_dim(near_pair, first_key, BAND, 1)
        key_global = base_row + first_key + jnp.arange(BAND, dtype=jnp.int32)
        row_local = block_index * CB + jnp.arange(CB, dtype=jnp.int32)
        queries = lax.dynamic_slice_in_dim(coarse_queries, block_index * CB, CB, 0)
        return cross_attend(
            queries,
            keys_block[0],
            keys_block[1],
            key_global,
            band_low,
            band_high,
            stream_start + row_local,
            slopes,
            row_local < live_count,
        )

    stacked = jax.vmap(coarse_block)(jnp.arange(block_total, dtype=jnp.int32))
    return stacked.reshape(coarse_queries.shape[0], coarse_queries.shape[1])


def solution(mesh):
    return jax.shard_map(
        on_device,
        mesh=mesh,
        in_specs=(
            P(("groups", "ctx"), None),
            P(("groups", "ctx"), None),
            P(("groups", "ctx"), None),
            P(("groups", "ctx"), None),
            P("ctx", None),
            P(),
            P("ctx", None),
            P("ctx", None),
            P(),
            P(("groups", "ctx"), None),
            P(("groups", "ctx")),
            P(("groups", "ctx"), None),
        ),
        out_specs=P(("groups", "ctx"), None),
        check_vma=False,
    )
```

profile of v0, /device:TPU:9, one launch (start us, length us, event | category | flops | bytes accessed | tf_op | source)
XLA Modules:
  0.0 288.7 jit_solution(17727069789186815152)
XLA Ops:
  6.6 0.7 all-gather.5.cloned.1.call-update
  7.3 0.7 all-gather.7.cloned.1.call-update
  8.1 0.7 all-gather.9.cloned.1.call-update
  8.8 1.2 copy.19
  10.0 1.2 copy.20
  11.4 3.1 %collective-permute-start = (bf16[2,256,1024]{1,2,0:T(8,128)(2,1)S(1)}, bf16[2,256,1024]{1,2,0:T(8,128)(2,1)}, u32[]{:S(2)}, u32[]{:S(2)}) collective-permute-start(bf16[2,256,1024]{1,2,0:T(8,128)(2,1)S(1)} %pad_maximum_fusion.1), channel_id=1, source_target_pairs={{0,2},{1,3},{2,4},{3,5},{4,6},{5,7},{6,8},{7,9},{8,10},{9,11},{10,... | collective-permute-start | bytes 3145736 | tf_op jit(solution)/shard_map/ppermute | solution.py:19
  15.8 0.8 dynamic-update-slice.4
  16.5 4.0 %collective-permute-start.1 = (bf16[2,256,1024]{1,2,0:T(8,128)(2,1)S(1)}, bf16[2,256,1024]{1,2,0:T(8,128)(2,1)}, u32[]{:S(2)}, u32[]{:S(2)}) collective-permute-start(bf16[2,256,1024]{1,2,0:T(8,128)(2,1)S(1)} %pad_maximum_fusion.1), channel_id=1, source_target_pairs={{0,1},{1,2},{2,3},{3,4},{4,5},{5,6},{6,7},{7,8},{8,9},{9,10},{10,1... | collective-permute-start | bytes 3145736 | tf_op jit(solution)/shard_map/ppermute | solution.py:19
  20.5 42.3 %all-reduce.1 = s32[16]{0:T(128)S(1)} all-reduce(s32[16]{0:T(128)S(1)} %dynamic-update-slice.4), channel_id=2, replica_groups=mesh['groups'=2,'ctx'=16] {'ctx'}, use_global_device_ids=true, to_apply=%add.1 | all-reduce | flops 16 | bytes 128
  64.3 20.7 %while.15 = (s32[]{:T(128)}, s32[1]{0:T(128)}, s32[]{:T(128)}, s32[16,1]{0,1:T(1,128)S(1)}, s32[]{:T(128)}) while((s32[]{:T(128)}, s32[1]{0:T(128)}, s32[]{:T(128)}, s32[16,1]{0,1:T(1,128)S(1)}, s32[]{:T(128)}) %tuple.70), condition=%wide.region_4.5_spmd, body=%wide.region_3.4_spmd.sunk | while | flops 5 | bytes 107 | solution.py:32
  65.6 0.6 constant_dynamic-slice_fusion.6
  66.9 0.6 constant_dynamic-slice_fusion.6
  68.2 0.6 constant_dynamic-slice_fusion.6
  69.5 0.6 constant_dynamic-slice_fusion.6
  85.6 1.5 subtract_abs_fusion
  87.1 1.7 maximum_maximum_fusion
  89.0 1.0 fusion.35
  90.1 3.1 %fusion.66 = (f32[8,256]{1,0:T(8,128)S(1)}, f32[8,256,768]{1,2,0:T(8,128)S(1)}) fusion(f32[8,768,256]{2,1,0:T(8,128)S(1)} %fusion.35, pred[256,768]{0,1:T(8,128)(4,1)S(1)} %fusion.34), kind=kOutput, calls=%fused_computation.93 | output fusion | flops 9437951 | bytes 12787712 | tf_op jit(solution)/shard_map/sub | solution.py:61
  93.8 3.9 %multiply_reduce_fusion = (f32[256]{0:T(256)S(1)}, f32[256,2048]{1,0:T(8,128)S(1)}) fusion(bf16[256,1024]{0,1:T(8,128)(2,1)S(1)} %bitcast.109, bf16[1024,2048]{1,0:T(8,128)(2,1)} %all-gather.5.cloned.1.call-done, bf16[256,2048]{1,0:T(8,128)(2,1)} %param.17), kind=kOutput, calls=%fused_computation.38 | convolution fusion | flops 1075838720 | bytes 7865344 | tf_op jit(solution)/shard_map/dot_general | solution.py:89
  97.7 27.9 %all-gather.7.cloned.1.call-done = bf16[2048,1024]{1,0:T(8,128)(2,1)} async-done(((bf16[128,1024]{1,0:T(8,128)(2,1)}), bf16[2048,1024]{1,0:T(8,128)(2,1)}) %all-gather.7.cloned.1.call-update) | async-done | bytes 4194320 | tf_op jit(solution)/shard_map/all_gather | solution.py:127
  125.6 3.5 %fusion.29 = bf16[1,256,1024]{2,1,0:T(8,128)(2,1)S(1)} fusion(bf16[2048,1024]{1,0:T(8,128)(2,1)} %all-gather.7.cloned.1.call-done, f32[256,2048]{1,0:T(8,128)S(1)} %get-tuple-element.138, f32[2048]{0:T(1024)S(1)} %copy-done.9, f32[256]{0:T(256)S(1)} %add_rsqrt_fusion), kind=kOutput, calls=%fused_computation.44 | convolution fusion | flops 1075576832 | bytes 6824960 | tf_op jit(solution)/shard_map/dot_general | solution.py:89
  129.1 47.7 %all-gather.9.cloned.1.call-done = bf16[2048,1024]{1,0:T(8,128)(2,1)} async-done(((bf16[128,1024]{1,0:T(8,128)(2,1)}), bf16[2048,1024]{1,0:T(8,128)(2,1)}) %all-gather.9.cloned.1.call-update) | async-done | bytes 4194320 | tf_op jit(solution)/shard_map/all_gather | solution.py:128
  176.9 3.5 %fusion.30 = bf16[1,256,1024]{2,1,0:T(8,128)(2,1)S(1)} fusion(bf16[2048,1024]{1,0:T(8,128)(2,1)} %all-gather.9.cloned.1.call-done, f32[256,2048]{1,0:T(8,128)S(1)} %get-tuple-element.138, f32[2048]{0:T(1024)S(1)} %copy-done.9, f32[256]{0:T(256)S(1)} %add_rsqrt_fusion), kind=kOutput, calls=%fused_computation.45 | convolution fusion | flops 1075576832 | bytes 6824960 | tf_op jit(solution)/shard_map/dot_general | solution.py:89
  180.5 2.3 collective-permute-start.2
  182.8 2.2 collective-permute-start.3
  185.1 12.5 %while.17 = (s32[]{:T(128)}, bf16[1024,1024]{1,0:T(8,128)(2,1)}, s32[4,2]{0,1:T(2,128)S(1)}, bf16[4,256,1024]{2,1,0:T(8,128)(2,1)}, s32[]{:T(128)}) while((s32[]{:T(128)}, bf16[1024,1024]{1,0:T(8,128)(2,1)}, s32[4,2]{0,1:T(2,128)S(1)}, bf16[4,256,1024]{2,1,0:T(8,128)(2,1)}, s32[]{:T(128)}) %tuple.61), condition=%wide.while_cond.1, body=%wide.while_body.1.sunk | while | flops 2 | bytes 1049689 | solution.py:145
  185.7 2.5 bitcast_dynamic-update-slice_fusion.5
  188.8 2.5 bitcast_dynamic-update-slice_fusion.5
  191.9 2.6 bitcast_dynamic-update-slice_fusion.5
  195.1 2.5 bitcast_dynamic-update-slice_fusion.5
  197.6 8.2 %collective-permute-done.2 = bf16[2,256,1024]{2,1,0:T(8,128)(2,1)S(1)} collective-permute-done((bf16[2,256,1024]{2,1,0:T(8,128)(2,1)S(1)}, bf16[2,256,1024]{2,1,0:T(8,128)(2,1)S(1)}, u32[]{:S(2)}, u32[]{:S(2)}) %collective-permute-start.2) | collective-permute-done | bytes 1048608 | tf_op jit(solution)/shard_map/ppermute | solution.py:42
  205.8 1.0 copy-done.7
  206.7 1.7 collective-permute-done.3
  208.4 2.1 pad_maximum_fusion
  210.5 12.7 %while.16 = (s32[]{:T(128)}, bf16[2,768,1024]{2,1,0:T(8,128)(2,1)S(1)}, s32[4,3]{1,0:T(4,128)S(1)}, bf16[4,2,512,1024]{3,2,1,0:T(8,128)(2,1)}, s32[]{:T(128)}) while((s32[]{:T(128)}, bf16[2,768,1024]{2,1,0:T(8,128)(2,1)S(1)}, s32[4,3]{1,0:T(4,128)S(1)}, bf16[4,2,512,1024]{3,2,1,0:T(8,128)(2,1)}, s32[]{:T(128)}) %tuple.55), condition=%wide.while_cond, body=%wide.while_body.sunk | while | flops 2 | bytes 4195425 | solution.py:142
  211.2 2.5 bitcast_dynamic-update-slice_fusion.4
  214.3 2.5 bitcast_dynamic-update-slice_fusion.4
  217.5 2.6 bitcast_dynamic-update-slice_fusion.4
  220.6 2.6 bitcast_dynamic-update-slice_fusion.4
  223.2 11.5 %copy.26 = bf16[4,2,512,1024]{2,3,0,1:T(8,128)(2,1)} copy(bf16[4,2,512,1024]{3,2,1,0:T(8,128)(2,1)} %get-tuple-element.92) | data formatting | bytes 16777216 | tf_op jit(solution)/shard_map/vmap()/gather | solution.py:142
  234.7 4.9 %slice.14 = bf16[4,1,512,1024]{3,2,1,0:T(8,128)(2,1)} slice(bf16[4,2,512,1024]{3,2,1,0:T(8,128)(2,1)} %get-tuple-element.92), slice={[0:4], [1:2], [0:512], [0:1024]} | slice | bytes 8388608 | tf_op jit(solution)/shard_map/vmap()/slice | solution.py:149
  239.7 1.2 copy-done.3
  240.9 2.2 slice.48
  243.1 6.4 %copy.25 = bf16[4,1,512,1024]{2,3,0,1:T(8,128)(2,1)} copy(bf16[4,1,512,1024]{3,2,1,0:T(8,128)(2,1)} %slice.14) | data formatting | bytes 8388608 | tf_op jit(solution)/shard_map/vmap()/slice | solution.py:149
  249.5 8.7 %fusion.67 = f32[4,8,256]{2,1,0:T(8,128)S(1)} fusion(f32[4,256,512]{2,1,0:T(8,128)S(1)} %copy-done.4, f32[8]{0:T(128)S(1)} %neg.4, pred[4,512]{1,0:T(4,128)(4,1)S(1)} %fusion.45, bf16[4,512,8,128]{1,3,2,0:T(8,128)(2,1)} %bitcast.106, bf16[4,256,1024]{2,1,0:T(8,128)(2,1)} %get-tuple-element.100), kind=kOutput, calls=%fused_computation.94 | convolution fusion | flops 1103102464 | bytes 8423456 | tf_op jit(solution)/shard_map/vmap()/sub | solution.py:61
  258.2 19.1 %fusion.16 = bf16[4,256,8,128]{1,3,2,0:T(8,128)(2,1)} fusion(bf16[4,512,8,128]{1,3,2,0:T(8,128)(2,1)} %bitcast.108, f32[4,8,256]{2,1,0:T(8,128)S(1)} %fusion.67, f32[4,256,512]{2,1,0:T(8,128)S(1)} %copy-done.4, f32[8]{0:T(128)S(1)} %neg.4, pred[4,512]{1,0:T(4,128)(4,1)S(1)} %fusion.45, bf16[4,512,8,128]{1,3,2,0:T(8,128)(2,1)} %bitcast.107, ...), kind=kOutput, calls=%fused_computation.33 | convolution fusion | flops 2181046784 | bytes 14714912 | tf_op jit(solution)/shard_map/vmap(hqk,khd->qhd)/dot_general | solution.py:63
  277.3 3.1 %copy.29 = bf16[4,256,8,128]{3,2,1,0:T(8,128)(2,1)S(1)} copy(bf16[4,256,8,128]{1,3,2,0:T(8,128)(2,1)} %fusion.16) | data formatting | bytes 4194304 | tf_op jit(solution)/shard_map/vmap(hqk,khd->qhd)/transpose | solution.py:63
  280.4 1.7 fusion.11
  (85 shorter events, 16.3 us)
Async XLA Ops:
  6.5 82.5 %copy-start = (bf16[256,1024]{1,0:T(8,128)(2,1)S(1)}, bf16[256,1024]{1,0:T(8,128)(2,1)}, u32[]{:S(2)}) copy-start(bf16[256,1024]{1,0:T(8,128)(2,1)} %param.14) | copy-start | bytes 1572868
  6.5 8.6 %copy-start.11 = (u32[32]{0:T(128)S(1)}, u32[32]{0:T(128)}, u32[]{:S(2)}) copy-start(u32[32]{0:T(128)} %constant.166) | copy-start | bytes 388
  6.5 57.1 %copy-start.8 = (s32[4]{0:T(128)S(1)}, s32[4]{0:T(128)}, u32[]{:S(2)}) copy-start(s32[4]{0:T(128)} %constant.163) | copy-start | bytes 52
  6.5 56.3 %copy-start.2 = (s32[4,2]{0,1:T(2,128)S(1)}, s32[4,2]{0,1:T(2,128)}, u32[]{:S(2)}) copy-start(s32[4,2]{0,1:T(2,128)} %param.25) | copy-start | bytes 100
  6.5 87.3 %all-gather.5.cloned.1.call-start = ((), (), s32[]{:S(2)}) async-start(), calls=%async_computation | async-start | bytes 4456448 | tf_op jit(solution)/shard_map/all_gather | solution.py:124
  7.3 118.3 %all-gather.7.cloned.1.call-start = ((), (), s32[]{:S(2)}) async-start(), calls=%async_computation.1 | async-start | bytes 4456448 | tf_op jit(solution)/shard_map/all_gather | solution.py:127
  8.0 168.9 %all-gather.9.cloned.1.call-start = ((), (), s32[]{:S(2)}) async-start(), calls=%async_computation.2 | async-start | bytes 4456448 | tf_op jit(solution)/shard_map/all_gather | solution.py:128
  11.4 75.8 %collective-permute-start = (bf16[2,256,1024]{1,2,0:T(8,128)(2,1)S(1)}, bf16[2,256,1024]{1,2,0:T(8,128)(2,1)}, u32[]{:S(2)}, u32[]{:S(2)}) collective-permute-start(bf16[2,256,1024]{1,2,0:T(8,128)(2,1)S(1)} %pad_maximum_fusion.1), channel_id=1, source_target_pairs={{0,2},{1,3},{2,4},{3,5},{4,6},{5,7},{6,8},{7,9},{8,10},{9,11},{10,... | collective-permute-start | bytes 3145736 | tf_op jit(solution)/shard_map/ppermute | solution.py:19
  16.5 70.6 %collective-permute-start.1 = (bf16[2,256,1024]{1,2,0:T(8,128)(2,1)S(1)}, bf16[2,256,1024]{1,2,0:T(8,128)(2,1)}, u32[]{:S(2)}, u32[]{:S(2)}) collective-permute-start(bf16[2,256,1024]{1,2,0:T(8,128)(2,1)S(1)} %pad_maximum_fusion.1), channel_id=1, source_target_pairs={{0,1},{1,2},{2,3},{3,4},{4,5},{5,6},{6,7},{7,8},{8,9},{9,10},{10,1... | collective-permute-start | bytes 3145736 | tf_op jit(solution)/shard_map/ppermute | solution.py:19
  93.8 31.8 %copy-start.9 = (f32[2048]{0:T(1024)S(1)}, f32[2048]{0:T(1024)}, u32[]{:S(2)}) copy-start(f32[2048]{0:T(1024)} %param.19) | copy-start | bytes 24580
  129.1 51.4 %copy-start.5 = (bf16[1,256,1024]{2,1,0:T(8,128)(2,1)}, bf16[1,256,1024]{2,1,0:T(8,128)(2,1)S(1)}, u32[]{:S(2)}) copy-start(bf16[1,256,1024]{2,1,0:T(8,128)(2,1)S(1)} %fusion.29) | copy-start | bytes 1572868
  129.1 55.9 %copy-start.10 = (f32[8]{0:T(128)S(1)}, f32[8]{0:T(128)}, u32[]{:S(2)}) copy-start(f32[8]{0:T(128)} %param.22) | copy-start | bytes 100
  180.4 2.4 copy-start.6
  180.5 25.3 %collective-permute-start.2 = (bf16[2,256,1024]{2,1,0:T(8,128)(2,1)S(1)}, bf16[2,256,1024]{2,1,0:T(8,128)(2,1)S(1)}, u32[]{:S(2)}, u32[]{:S(2)}) collective-permute-start(bf16[2,256,1024]{2,1,0:T(8,128)(2,1)S(1)} %pad_maximum_fusion.2), channel_id=1, source_target_pairs={{0,1},{1,2},{2,3},{3,4},{4,5},{5,6},{6,7},{7,8},{8,9},{9,10},{10,1... | collective-permute-start | bytes 3145736 | tf_op jit(solution)/shard_map/ppermute | solution.py:42
  182.8 25.6 %collective-permute-start.3 = (bf16[2,256,1024]{2,1,0:T(8,128)(2,1)S(1)}, bf16[2,256,1024]{2,1,0:T(8,128)(2,1)}, u32[]{:S(2)}, u32[]{:S(2)}) collective-permute-start(bf16[2,256,1024]{2,1,0:T(8,128)(2,1)S(1)} %pad_maximum_fusion.2), channel_id=1, source_target_pairs={{1,0},{2,1},{3,2},{4,3},{5,4},{6,5},{7,6},{8,7},{9,8},{10,9},{11,1... | collective-permute-start | bytes 3145736 | tf_op jit(solution)/shard_map/ppermute | solution.py:43
  205.8 1.0 copy-start.7
  234.7 6.2 %copy-start.3 = (bf16[4,2,512,1024]{2,3,0,1:T(8,128)(2,1)S(1)}, bf16[4,2,512,1024]{2,3,0,1:T(8,128)(2,1)}, u32[]{:S(2)}) copy-start(bf16[4,2,512,1024]{2,3,0,1:T(8,128)(2,1)} %copy.26) | copy-start | bytes 25165828
  243.1 6.4 %copy-start.4 = (f32[4,256,512]{2,1,0:T(8,128)S(1)}, f32[4,256,512]{2,1,0:T(8,128)}, u32[]{:S(2)}) copy-start(f32[4,256,512]{2,1,0:T(8,128)} %subtract_abs_fusion) | copy-start | bytes 6291460
  258.2 24.0 %copy-start.1 = (bf16[256,1024]{1,0:T(8,128)(2,1)S(1)}, bf16[256,1024]{1,0:T(8,128)(2,1)}, u32[]{:S(2)}) copy-start(bf16[256,1024]{1,0:T(8,128)(2,1)} %param.14) | copy-start | bytes 1572868
Sparse Core Ops, SparseCore 0:
  9.5 62.7 all-gather.4
  74.5 51.1 all-gather.6
  127.8 49.0 all-gather.8
where the time goes:
time: 290 us; the launch traced here: 289 us
  waiting for transfers between devices  87.6 us (30%)
  local copies, waits for them, and re-layouts  71.4 us (25%)
  blocking collectives  42.3 us (15%)
  matrix products  40.3 us (14%)
  between operations  14.1 us (5%)
  starting transfers between devices  11.7 us (4%)
  other arithmetic  10.9 us (4%)
  loops' own time  10.4 us (4%)
    all_gather x1, waiting for transfers between devices, on_device(): lax.all_gather(value_proj, 'ctx', axis=0, tiled=True)  47.7 us
    unnamed x1, blocking collectives  42.3 us
    all_gather x1, waiting for transfers between devices, on_device(): lax.all_gather(key_proj, 'ctx', axis=0, tiled=True)  27.9 us
    gather x24, local copies, waits for them, and re-layouts  25.1 us
    dot_general x2, matrix products, attend(): jnp.einsum('hqk,khd->qhd', weights, head_split(value_rows), preferred_ele...  19.7 us
    gather x1, local copies, waits for them, and re-layouts, coarse_block(): keys_block = lax.dynamic_slice_in_dim(near_pair, first_key, BAND, 1)  11.5 us
    slice x2, local copies, waits for them, and re-layouts, coarse_block(): keys_block[1]  11.3 us
    dot_general x3, matrix products, contract_rows(): return jnp.dot(left_side, weight_piece, preferred_element_type=jnp.float32)  10.8 us
  transfers between devices with their start and end apart: 7, of which 4 were waited for; matrix products, arithmetic and copies ran while one was open for 15% of the time, Pallas kernels for 0%

commit v1 on v0

--- a/solution.py
+++ b/solution.py
@@ -1,6 +1,8 @@
 import jax
 import jax.numpy as jnp
 from jax import lax
+from jax.experimental import pallas as pl
+from jax.experimental.pallas import tpu as pltpu
 from jax.sharding import PartitionSpec as P
 
 HEADS = 8
@@ -73,16 +75,62 @@
     return (scaled * norm_gain[None, :]).astype(jnp.bfloat16)
 
 
-def cross_attend(
-    queries, key_rows, value_rows, key_global, band_low, band_high, positions, slopes, live_rows
-):
-    timing = (positions // 2).astype(jnp.float32) * (2.0 / 3.0)
-    distance = jnp.abs(timing[:, None] - key_global[None, :].astype(jnp.float32))
-    time_bias = -slopes[:, None, None] * distance[None] / BAND
-    inside = (key_global >= band_low) & (key_global < band_high)
-    allowed = jnp.broadcast_to(inside[None, :], (queries.shape[0], key_global.shape[0]))
-    blended = attend(queries, key_rows, value_rows, allowed, time_bias)
-    return jnp.where(live_rows[:, None], blended, 0.0).astype(jnp.bfloat16)
+LOG2E = 1.4426950408889634
+SCALE2 = HEAD_DIM ** (-0.5) * LOG2E
+SPAN = BAND + 16
+MASKED = 1e30
+
+
+def cross_kernel(bounds, meta, slopes, q_ref, k_ref, v_ref, o_ref, dist_ref):
+    block = pl.program_id(0)
+    stream_start, live, base = meta[0], meta[1], meta[2]
+    low, high = bounds[block, 0], bounds[block, 1]
+    near_rows = k_ref.shape[0]
+    first = jnp.minimum((low - base) // 16 * 16, near_rows - SPAN)
+    first = pl.multiple_of(first, 16)
+    rows = pl.ds(first, SPAN)
+    row_local = block * CB + lax.broadcasted_iota(jnp.int32, (1, CB), 1)
+    timing = ((stream_start + row_local) // 2).astype(jnp.float32) * (2.0 / 3.0)
+    key_global = base + first + lax.broadcasted_iota(jnp.int32, (SPAN, CB), 0)
+    distance = jnp.abs(timing - key_global.astype(jnp.float32))
+    inside = (key_global >= low) & (key_global < high)
+    dist_ref[...] = jnp.where(inside, distance, MASKED)
+    live_row = row_local < live
+    for head in range(HEADS):
+        cols = slice(head * HEAD_DIM, (head + 1) * HEAD_DIM)
+        scores = lax.dot_general(
+            k_ref[rows, cols], q_ref[:, cols], (((1,), (1,)), ((), ())),
+            preferred_element_type=jnp.float32,
+        )
+        scores = scores * SCALE2 - dist_ref[...] * (slopes[head] * (LOG2E / BAND))
+        exponent = jnp.exp2(scores - jnp.max(scores, axis=0, keepdims=True))
+        total = jnp.sum(exponent, axis=0, keepdims=True)
+        blended = lax.dot_general(
+            v_ref[rows, cols], exponent.astype(jnp.bfloat16), (((0,), (0,)), ((), ())),
+            preferred_element_type=jnp.float32,
+        )
+        blended = jnp.where(live_row, blended / total, 0.0)
+        o_ref[:, cols] = blended.T.astype(jnp.bfloat16)
+
+
+def cross_attention(bounds, meta, slopes, queries, near_keys, near_values):
+    blocks, width = bounds.shape[0], queries.shape[1]
+    whole = pl.BlockSpec(near_keys.shape, lambda b: (0, 0))
+    smem = pl.BlockSpec(memory_space=pltpu.SMEM)
+    return pl.pallas_call(
+        cross_kernel,
+        grid=(blocks,),
+        in_specs=[smem, smem, smem, pl.BlockSpec((CB, width), lambda b: (b, 0)), whole, whole],
+        out_specs=pl.BlockSpec((CB, width), lambda b: (b, 0)),
+        out_shape=jax.ShapeDtypeStruct(queries.shape, jnp.bfloat16),
+        scratch_shapes=[pltpu.VMEM((SPAN, CB), jnp.float32)],
+        compiler_params=pltpu.CompilerParams(vmem_limit_bytes=48 * 1024 * 1024),
+        cost_estimate=pl.CostEstimate(
+            flops=4 * queries.shape[0] * SPAN * width, bytes_accessed=8 * 1024 * 1024,
+            transcendentals=queries.shape[0] * SPAN * HEADS,
+        ),
+        name="cross_attention",
+    )(bounds, meta, slopes, queries, near_keys, near_values)
 
 
 def contract_rows(left_side, weight_piece):
@@ -131,32 +179,8 @@
     stream_start = carried_in(counts, "ctx", add_counts, jnp.zeros_like(counts))[0]
     near_pair = with_halo(jnp.stack([cross_keys, cross_values]), (("ctx", 1),), rows_here)
     base_row = (device_index - 1) * rows_here
-    live_count = counts[0]
-    near_rows = near_pair.shape[1]
-    block_total = band_bounds.shape[0]
-
-    def coarse_block(block_index):
-        band_low = band_bounds[block_index, 0]
-        band_high = band_bounds[block_index, 1]
-        first_key = jnp.minimum(band_low - base_row, near_rows - BAND)
-        keys_block = lax.dynamic_slice_in_dim(near_pair, first_key, BAND, 1)
-        key_global = base_row + first_key + jnp.arange(BAND, dtype=jnp.int32)
-        row_local = block_index * CB + jnp.arange(CB, dtype=jnp.int32)
-        queries = lax.dynamic_slice_in_dim(coarse_queries, block_index * CB, CB, 0)
-        return cross_attend(
-            queries,
-            keys_block[0],
-            keys_block[1],
-            key_global,
-            band_low,
-            band_high,
-            stream_start + row_local,
-            slopes,
-            row_local < live_count,
-        )
-
-    stacked = jax.vmap(coarse_block)(jnp.arange(block_total, dtype=jnp.int32))
-    return stacked.reshape(coarse_queries.shape[0], coarse_queries.shape[1])
+    meta = jnp.stack([stream_start, counts[0], base_row]).astype(jnp.int32)
+    return cross_attention(band_bounds, meta, slopes, coarse_queries, near_pair[0], near_pair[1])
 
 
 def solution(mesh):

time: 290 us -> 264 us (0.910)
  the two profiles are of different devices: /device:TPU:9 before, /device:TPU:0 now
where the time goes in v1:
time: 264 us; the launch traced here: 263 us
  waiting for transfers between devices  146 us (55%)
  blocking collectives  27.4 us (10%)
  Pallas kernels  16.9 us (6%)
  local copies, waits for them, and re-layouts  15.5 us (6%)
  between operations  14 us (5%)
  matrix products  13.2 us (5%)
  starting transfers between devices  12.9 us (5%)
  loops' own time  10.5 us (4%)
  other arithmetic  7.02 us (3%)
    all_gather x1, waiting for transfers between devices, on_device(): lax.all_gather(value_proj, 'ctx', axis=0, tiled=True)  47.7 us
    all_gather x1, waiting for transfers between devices, on_device(): lax.all_gather(key_proj, 'ctx', axis=0, tiled=True)  47.6 us
    unnamed x1, blocking collectives  27.4 us
    all_gather x1, waiting for transfers between devices, on_device(): lax.all_gather(out_proj, 'ctx', axis=0, tiled=True)  26 us
    ppermute x2, waiting for transfers between devices, passed_along(): return lax.ppermute(array, axis, pairs)  22.6 us
    pallas_call x1, Pallas kernels, cross_attention(): pl.pallas_call(cross_kernel, grid=(blocks,), in_specs=[smem, smem, smem,...  16.9 us
    dot_general x3, matrix products, contract_rows(): return jnp.dot(left_side, weight_piece, preferred_element_type=jnp.float32)  11.5 us
    another operation x1, loops' own time, carried_in(): return lax.fori_loop(0, length, step, start)  10.5 us
  transfers between devices with their start and end apart: 7, of which 4 were waited for; matrix products, arithmetic and copies ran while one was open for 11% of the time, Pallas kernels for 0%

profile of v1, /device:TPU:0, one launch (start us, length us, event | category | flops | bytes accessed | tf_op | source)
XLA Modules:
  0.0 263.3 jit_solution(6594067177170822052)
XLA Ops:
  6.5 0.7 all-gather.5.cloned.1.call-update
  7.3 0.7 all-gather.7.cloned.1.call-update
  8.1 0.7 all-gather.9.cloned.1.call-update
  8.7 1.2 copy.17
  10.0 1.2 copy.18
  11.2 0.1 pad_maximum_fusion.1
  11.3 5.9 %collective-permute-start = (bf16[2,256,1024]{1,2,0:T(8,128)(2,1)S(1)}, bf16[2,256,1024]{1,2,0:T(8,128)(2,1)}, u32[]{:S(2)}, u32[]{:S(2)}) collective-permute-start(bf16[2,256,1024]{1,2,0:T(8,128)(2,1)S(1)} %pad_maximum_fusion.1), channel_id=1, source_target_pairs={{0,2},{1,3},{2,4},{3,5},{4,6},{5,7},{6,8},{7,9},{8,10},{9,11},{10,... | collective-permute-start | bytes 3145736 | tf_op jit(solution)/shard_map/ppermute | solution.py:21
  17.2 2.5 collective-permute-start.1
  19.7 0.2 fusion.12
  20.0 22.6 %collective-permute-done = bf16[2,256,1024]{1,2,0:T(8,128)(2,1)} collective-permute-done((bf16[2,256,1024]{1,2,0:T(8,128)(2,1)S(1)}, bf16[2,256,1024]{1,2,0:T(8,128)(2,1)}, u32[]{:S(2)}, u32[]{:S(2)}) %collective-permute-start) | collective-permute-done | bytes 1048608 | tf_op jit(solution)/shard_map/ppermute | solution.py:21
  42.6 1.6 maximum_maximum_fusion
  44.2 0.2 fusion.18
  44.5 1.0 fusion.13
  45.5 3.1 %fusion.19 = (f32[8,256]{1,0:T(8,128)S(1)}, f32[8,256,768]{1,2,0:T(8,128)S(1)}) fusion(f32[8,768,256]{2,1,0:T(8,128)S(1)} %fusion.13, pred[256,768]{0,1:T(8,128)(4,1)S(1)} %fusion.12), kind=kOutput, calls=%fused_computation.39 | output fusion | flops 9437951 | bytes 12787712 | tf_op jit(solution)/shard_map/sub | solution.py:63
  48.6 0.6 fusion.6
  49.2 26.0 %all-gather.5.cloned.1.call-done = bf16[1024,2048]{1,0:T(8,128)(2,1)} async-done(((bf16[64,2048]{1,0:T(8,128)(2,1)}), bf16[1024,2048]{1,0:T(8,128)(2,1)}) %all-gather.5.cloned.1.call-update) | async-done | bytes 4194320 | tf_op jit(solution)/shard_map/all_gather | solution.py:172
  75.2 3.9 %multiply_reduce_fusion = (f32[256]{0:T(256)S(1)}, f32[256,2048]{1,0:T(8,128)S(1)}) fusion(bf16[256,1024]{0,1:T(8,128)(2,1)S(1)} %bitcast.53, bf16[1024,2048]{1,0:T(8,128)(2,1)} %all-gather.5.cloned.1.call-done, bf16[256,2048]{1,0:T(8,128)(2,1)} %param.17), kind=kOutput, calls=%fused_computation.14 | convolution fusion | flops 1075838720 | bytes 7865344 | tf_op jit(solution)/shard_map/dot_general | solution.py:137
  79.1 47.6 %all-gather.7.cloned.1.call-done = bf16[2048,1024]{1,0:T(8,128)(2,1)} async-done(((bf16[128,1024]{1,0:T(8,128)(2,1)}), bf16[2048,1024]{1,0:T(8,128)(2,1)}) %all-gather.7.cloned.1.call-update) | async-done | bytes 4194320 | tf_op jit(solution)/shard_map/all_gather | solution.py:175
  126.7 3.5 %fusion.7 = bf16[1,256,1024]{2,1,0:T(8,128)(2,1)S(1)} fusion(bf16[2048,1024]{1,0:T(8,128)(2,1)} %all-gather.7.cloned.1.call-done, f32[256,2048]{1,0:T(8,128)S(1)} %get-tuple-element.100, f32[2048]{0:T(1024)S(1)} %copy-done.5, f32[256]{0:T(256)S(1)} %add_rsqrt_fusion), kind=kOutput, calls=%fused_computation.20 | convolution fusion | flops 1075576832 | bytes 6824960 | tf_op jit(solution)/shard_map/dot_general | solution.py:137
  130.2 47.7 %all-gather.9.cloned.1.call-done = bf16[2048,1024]{1,0:T(8,128)(2,1)} async-done(((bf16[128,1024]{1,0:T(8,128)(2,1)}), bf16[2048,1024]{1,0:T(8,128)(2,1)}) %all-gather.9.cloned.1.call-update) | async-done | bytes 4194320 | tf_op jit(solution)/shard_map/all_gather | solution.py:176
  177.9 4.1 %fusion.8 = bf16[1,256,1024]{2,1,0:T(8,128)(2,1)S(1)} fusion(bf16[2048,1024]{1,0:T(8,128)(2,1)} %all-gather.9.cloned.1.call-done, f32[256,2048]{1,0:T(8,128)} %copy-done.3, f32[2048]{0:T(1024)S(1)} %copy-done.5, f32[256]{0:T(256)S(1)} %add_rsqrt_fusion), kind=kOutput, calls=%fused_computation.21 | convolution fusion | flops 1075576832 | bytes 6824960 | tf_op jit(solution)/shard_map/dot_general | solution.py:137
  182.1 0.1 pad_maximum_fusion.2
  182.2 3.2 %collective-permute-start.2 = (bf16[2,256,1024]{2,1,0:T(8,128)(2,1)S(1)}, bf16[2,256,1024]{2,1,0:T(8,128)(2,1)}, u32[]{:S(2)}, u32[]{:S(2)}) collective-permute-start(bf16[2,256,1024]{2,1,0:T(8,128)(2,1)S(1)} %pad_maximum_fusion.2), channel_id=1, source_target_pairs={{0,1},{1,2},{2,3},{3,4},{4,5},{5,6},{6,7},{7,8},{8,9},{9,10},{10,1... | collective-permute-start | bytes 3145736 | tf_op jit(solution)/shard_map/ppermute | solution.py:44
  185.3 1.3 collective-permute-start.3
  187.3 0.6 dynamic-slice
  187.9 0.8 dynamic-update-slice
  188.6 27.4 %all-reduce = s32[16]{0:T(128)S(1)} all-reduce(s32[16]{0:T(128)S(1)} %dynamic-update-slice), channel_id=2, replica_groups=mesh['groups'=2,'ctx'=16] {'ctx'}, use_global_device_ids=true, to_apply=%add | all-reduce | flops 16 | bytes 128
  216.2 20.3 %while.13 = (s32[]{:T(128)}, s32[1]{0:T(128)}, s32[]{:T(128)}, s32[16,1]{0,1:T(1,128)S(1)}, s32[]{:T(128)}) while((s32[]{:T(128)}, s32[1]{0:T(128)}, s32[]{:T(128)}, s32[16,1]{0,1:T(1,128)S(1)}, s32[]{:T(128)}) %tuple.41), condition=%wide.region_1.2_spmd, body=%wide.region_0.1_spmd.sunk | while | flops 5 | bytes 107 | solution.py:34
  216.2 0.6 constant_dynamic-slice_fusion.2
  217.4 0.6 constant_dynamic-slice_fusion.2
  218.7 0.6 constant_dynamic-slice_fusion.2
  220.0 0.6 constant_dynamic-slice_fusion.2
  221.2 0.6 constant_dynamic-slice_fusion.2
  222.5 0.6 constant_dynamic-slice_fusion.2
  223.8 0.6 constant_dynamic-slice_fusion.2
  225.0 0.6 constant_dynamic-slice_fusion.2
  226.3 0.6 constant_dynamic-slice_fusion.2
  227.6 0.6 constant_dynamic-slice_fusion.2
  228.8 0.6 constant_dynamic-slice_fusion.2
  230.1 0.6 constant_dynamic-slice_fusion.2
  231.4 0.6 constant_dynamic-slice_fusion.2
  232.7 0.6 constant_dynamic-slice_fusion.2
  233.9 0.6 constant_dynamic-slice_fusion.2
  235.2 0.6 constant_dynamic-slice_fusion.2
  236.5 1.8 pad_maximum_fusion
  238.3 0.3 slice_bitcast_fusion
  238.7 1.3 copy-done.1
  239.9 16.9 %cross_attention.1 = bf16[1024,1024]{1,0:T(8,128)(2,1)} custom-call(s32[4,2]{1,0:T(4,128)S(1)} %copy.22.bounds, s32[3]{0:T(128)S(1)} %pad_add_fusion.meta, f32[8]{0:T(128)S(1)} %copy-done.2, bf16[1024,1024]{1,0:T(8,128)(2,1)S(1)} %copy-done.1, bf16[768,1024]{1,0:T(8,128)(2,1)S(1)} %get-tuple-element.94.k_ref, bf16[768,1024]{1,0:T(8,128)(2,1)S(1)} %get-tuple-element.93.v_ref), custom_call_target="tpu_custom_call" | custom-call | flops 2214592512 | bytes 8388608 | tf_op jit(solution)/shard_map/cross_attention/pallas_call | solution.py:120
  (25 shorter events, 0.3 us)
Async XLA Ops:
  6.5 37.9 %copy-start = (bf16[256,1024]{1,0:T(8,128)(2,1)S(1)}, bf16[256,1024]{1,0:T(8,128)(2,1)}, u32[]{:S(2)}) copy-start(bf16[256,1024]{1,0:T(8,128)(2,1)} %param.14) | copy-start | bytes 1572868
  6.5 68.7 %all-gather.5.cloned.1.call-start = ((), (), s32[]{:S(2)}) async-start(), calls=%async_computation | async-start | bytes 4456448 | tf_op jit(solution)/shard_map/all_gather | solution.py:172
  7.3 119.4 %all-gather.7.cloned.1.call-start = ((), (), s32[]{:S(2)}) async-start(), calls=%async_computation.1 | async-start | bytes 4456448 | tf_op jit(solution)/shard_map/all_gather | solution.py:175
  8.0 169.9 %all-gather.9.cloned.1.call-start = ((), (), s32[]{:S(2)}) async-start(), calls=%async_computation.2 | async-start | bytes 4456448 | tf_op jit(solution)/shard_map/all_gather | solution.py:176
  11.3 31.2 %collective-permute-start = (bf16[2,256,1024]{1,2,0:T(8,128)(2,1)S(1)}, bf16[2,256,1024]{1,2,0:T(8,128)(2,1)}, u32[]{:S(2)}, u32[]{:S(2)}) collective-permute-start(bf16[2,256,1024]{1,2,0:T(8,128)(2,1)S(1)} %pad_maximum_fusion.1), channel_id=1, source_target_pairs={{0,2},{1,3},{2,4},{3,5},{4,6},{5,7},{6,8},{7,9},{8,10},{9,11},{10,... | collective-permute-start | bytes 3145736 | tf_op jit(solution)/shard_map/ppermute | solution.py:21
  17.2 25.4 %collective-permute-start.1 = (bf16[2,256,1024]{1,2,0:T(8,128)(2,1)S(1)}, bf16[2,256,1024]{1,2,0:T(8,128)(2,1)}, u32[]{:S(2)}, u32[]{:S(2)}) collective-permute-start(bf16[2,256,1024]{1,2,0:T(8,128)(2,1)S(1)} %pad_maximum_fusion.1), channel_id=1, source_target_pairs={{0,1},{1,2},{2,3},{3,4},{4,5},{5,6},{6,7},{7,8},{8,9},{9,10},{10,1... | collective-permute-start | bytes 3145736 | tf_op jit(solution)/shard_map/ppermute | solution.py:21
  75.2 51.5 %copy-start.5 = (f32[2048]{0:T(1024)S(1)}, f32[2048]{0:T(1024)}, u32[]{:S(2)}) copy-start(f32[2048]{0:T(1024)} %param.19) | copy-start | bytes 24580
  79.1 51.1 %copy-start.3 = (f32[256,2048]{1,0:T(8,128)}, f32[256,2048]{1,0:T(8,128)S(1)}, u32[]{:S(2)}) copy-start(f32[256,2048]{1,0:T(8,128)S(1)} %get-tuple-element.100) | copy-start | bytes 6291460
  130.2 57.1 %copy-start.6 = (u32[32]{0:T(128)S(1)}, u32[32]{0:T(128)}, u32[]{:S(2)}) copy-start(u32[32]{0:T(128)} %constant.60) | copy-start | bytes 388
  130.2 85.9 %copy-start.4 = (s32[4,2]{0,1:T(2,128)S(1)}, s32[4,2]{0,1:T(2,128)}, u32[]{:S(2)}) copy-start(s32[4,2]{0,1:T(2,128)} %param.25) | copy-start | bytes 100
  182.2 54.4 %collective-permute-start.2 = (bf16[2,256,1024]{2,1,0:T(8,128)(2,1)S(1)}, bf16[2,256,1024]{2,1,0:T(8,128)(2,1)}, u32[]{:S(2)}, u32[]{:S(2)}) collective-permute-start(bf16[2,256,1024]{2,1,0:T(8,128)(2,1)S(1)} %pad_maximum_fusion.2), channel_id=1, source_target_pairs={{0,1},{1,2},{2,3},{3,4},{4,5},{5,6},{6,7},{7,8},{8,9},{9,10},{10,1... | collective-permute-start | bytes 3145736 | tf_op jit(solution)/shard_map/ppermute | solution.py:44
  185.3 51.2 %collective-permute-start.3 = (bf16[2,256,1024]{2,1,0:T(8,128)(2,1)S(1)}, bf16[2,256,1024]{2,1,0:T(8,128)(2,1)}, u32[]{:S(2)}, u32[]{:S(2)}) collective-permute-start(bf16[2,256,1024]{2,1,0:T(8,128)(2,1)S(1)} %pad_maximum_fusion.2), channel_id=1, source_target_pairs={{1,0},{2,1},{3,2},{4,3},{5,4},{6,5},{7,6},{8,7},{9,8},{10,9},{11,1... | collective-permute-start | bytes 3145736 | tf_op jit(solution)/shard_map/ppermute | solution.py:45
  238.3 1.6 copy-start.1
  238.3 1.6 copy-start.2
Sparse Core Ops, SparseCore 0:
  9.5 65.6 all-gather.4
  77.4 49.2 all-gather.6
  128.8 49.0 all-gather.8

commit v2 on v1

v2 whole, which is shorter than its diff:
```python
import functools

import jax
import jax.numpy as jnp
from jax import lax
from jax.experimental import pallas as pl
from jax.experimental.pallas import tpu as pltpu
from jax.sharding import PartitionSpec as P

HEADS = 8
HEAD_DIM = 128
W = 512
BAND = 512
CB = 256


LOG2E = 1.4426950408889634
SCALE2 = HEAD_DIM ** (-0.5) * LOG2E
SPAN = BAND + 16
MASKED = 1e30


def cross_kernel(bounds, start, counts, slopes, q_ref, k_ref, v_ref, o_ref, dist_ref):
    block = pl.program_id(0)
    stream_start, live = start[0, 0], counts[0]
    low, high = bounds[block, 0], bounds[block, 1]
    near_rows = k_ref.shape[0]
    base = (lax.axis_index("ctx") - 1) * (near_rows // 3)
    first = jnp.minimum((low - base) // 16 * 16, near_rows - SPAN)
    first = pl.multiple_of(first, 16)
    rows = pl.ds(first, SPAN)
    row_local = block * CB + lax.broadcasted_iota(jnp.int32, (1, CB), 1)
    timing = ((stream_start + row_local) // 2).astype(jnp.float32) * (2.0 / 3.0)
    key_global = base + first + lax.broadcasted_iota(jnp.int32, (SPAN, CB), 0)
    distance = jnp.abs(timing - key_global.astype(jnp.float32))
    inside = (key_global >= low) & (key_global < high)
    dist_ref[...] = jnp.where(inside, distance, MASKED)
    live_row = row_local < live
    for head in range(HEADS):
        cols = slice(head * HEAD_DIM, (head + 1) * HEAD_DIM)
        scores = lax.dot_general(
            k_ref[rows, cols], q_ref[:, cols], (((1,), (1,)), ((), ())),
            preferred_element_type=jnp.float32,
        )
        scores = scores * SCALE2 - dist_ref[...] * (slopes[head] * (LOG2E / BAND))
        exponent = jnp.exp2(scores - jnp.max(scores, axis=0, keepdims=True))
        total = jnp.sum(exponent, axis=0, keepdims=True)
        blended = lax.dot_general(
            v_ref[rows, cols], exponent.astype(jnp.bfloat16), (((0,), (0,)), ((), ())),
            preferred_element_type=jnp.float32,
        )
        blended = jnp.where(live_row, blended / total, 0.0)
        o_ref[:, cols] = blended.T.astype(jnp.bfloat16)


def cross_attention(bounds, start, counts, slopes, queries, near_keys, near_values):
    blocks, width = bounds.shape[0], queries.shape[1]
    whole = pl.BlockSpec(near_keys.shape, lambda b: (0, 0))
    smem = pl.BlockSpec(memory_space=pltpu.SMEM)
    return pl.pallas_call(
        cross_kernel,
        grid=(blocks,),
        in_specs=[smem, smem, smem, smem, pl.BlockSpec((CB, width), lambda b: (b, 0)), whole, whole],
        out_specs=pl.BlockSpec((CB, width), lambda b: (b, 0)),
        out_shape=jax.ShapeDtypeStruct(queries.shape, jnp.bfloat16),
        scratch_shapes=[pltpu.VMEM((SPAN, CB), jnp.float32)],
        compiler_params=pltpu.CompilerParams(vmem_limit_bytes=48 * 1024 * 1024),
        cost_estimate=pl.CostEstimate(
            flops=4 * queries.shape[0] * SPAN * width, bytes_accessed=8 * 1024 * 1024,
            transcendentals=queries.shape[0] * SPAN * HEADS,
        ),
        name="cross_attention",
    )(bounds, start, counts, slopes, queries, near_keys, near_values)


def ring_position(index, n):
    chips, chip, core = n // 2, index // 2, index % 2
    odd = chip % 2
    return ((1 - odd) * (chip // 2) + odd * (chips - 1 - chip // 2)) * 2 + core


def ring_index(position, n):
    position = (position + n) % n
    chips, place, core = n // 2, position // 2, position % 2
    back = place // (chips // 2)
    return ((1 - back) * 2 * place + back * (2 * (chips - 1 - place) + 1)) * 2 + core


def semantic_kernel(
    n, q_ref, k_ref, v_ref, x_ref, gain_ref, wo_ref, wk_ref, wv_ref, count_ref,
    near_k, near_v, start_ref,
    win_k, win_v, all_o, all_k, all_v, all_c, att, stream, normed, mask,
    ring_send, ring_recv, sem_send, sem_recv, near_send, near_recv,
):
    me = lax.axis_index("ctx")
    rows = q_ref.shape[0]
    reach = win_k.shape[0] // rows - 1
    spot = ring_position(me, n)
    after, before = ring_index(spot + 1, n), ring_index(spot + n - 1, n)
    steps = (n // 2, n - 1 - n // 2)

    barrier = pltpu.get_barrier_semaphore()
    partners = [after, before]
    for far in range(1, reach + 1):
        partners += [(me + far) % n, (me + n - far) % n]
    for partner in partners:
        pl.semaphore_signal(
            barrier, inc=1, device_id={"ctx": partner}, device_id_type=pl.DeviceIdType.MESH
        )
    pl.semaphore_wait(barrier, len(partners))

    def send(src, dst, sems, place, target):
        return pltpu.make_async_remote_copy(
            src_ref=src, dst_ref=dst, send_sem=sems[0].at[place], recv_sem=sems[1].at[place],
            device_id={"ctx": target}, device_id_type=pl.DeviceIdType.MESH,
        )

    half_o = all_o.shape[1] // 2
    pieces = [
        (all_o, slice(0, half_o)), (all_o, slice(half_o, 2 * half_o)), (all_c, slice(0, 128)),
        (all_k, slice(0, all_k.shape[1])), (all_v, slice(0, all_v.shape[1])),
    ]

    def ring(piece, way, step, arriving=False):
        ref, cols = pieces[piece]
        depth = ref.shape[0] // n
        back = step + 1 if arriving else step
        owner = ring_index(spot + n - back if way == 0 else spot + back, n)
        part = ref.at[pl.ds(pl.multiple_of(owner * depth, depth), depth), cols]
        place = (piece * 2 + way) * steps[0] + step
        return send(part, part, (ring_send, ring_recv), place, after if way == 0 else before)

    def begin(group):
        for piece in group:
            for way in (0, 1):
                ring(piece, way, 0).start()

    def forward(group, step):
        for piece in group:
            for way in (0, 1):
                ring(piece, way, step, True).wait_recv()
                ring(piece, way, step + 1).start()

    def finish(group):
        last = steps[0] - 1
        for piece in group:
            ring(piece, 0, last - 1, True).wait_recv()
            ring(piece, 0, last).start()
            ring(piece, 1, last - 1, True).wait_recv()
        for piece in group:
            ring(piece, 0, last, True).wait_recv()

    first_group, second_group = (0, 1, 2), (3, 4)
    for full, own in ((all_o, wo_ref), (all_k, wk_ref), (all_v, wv_ref), (all_c, count_ref)):
        depth = own.shape[0]
        full[pl.ds(pl.multiple_of(me * depth, depth), depth), :] = own[...]
    here = pl.ds(reach * rows, rows)
    win_k[here, :] = k_ref[...]
    win_v[here, :] = v_ref[...]

    def window_copies(far):
        there = pl.ds((reach - far) * rows, rows)
        target = (me + far) % n
        return [
            send(win.at[here], win.at[there], (sem_send, sem_recv), 2 * (far - 1) + i, target)
            for i, win in enumerate((win_k, win_v))
        ]

    def window_start(far):
        @pl.when(me + far < n)
        def _():
            for copy in window_copies(far):
                copy.start()

        @pl.when(me < far)
        def _():
            there = pl.ds((reach - far) * rows, rows)
            win_k[there, :] = jnp.zeros((rows, win_k.shape[1]), jnp.bfloat16)
            win_v[there, :] = jnp.zeros((rows, win_v.shape[1]), jnp.bfloat16)

    begin(first_group)
    for far in range(1, reach + 1):
        window_start(far)

    key_row = lax.broadcasted_iota(jnp.int32, mask.shape, 0)
    lag = lax.broadcasted_iota(jnp.int32, mask.shape, 1) + reach * rows - key_row
    allowed = (lag >= 0) & (lag < W) & (key_row + (me - reach) * rows >= 0)
    mask[...] = jnp.where(allowed, 0.0, -MASKED)

    def first_step(step, carry):
        forward(first_group, step)
        return carry

    lax.fori_loop(0, steps[0] - 2, first_step, 0)
    begin(second_group)
    finish(first_group)

    for far in range(1, reach + 1):
        @pl.when(me >= far)
        def _():
            for copy in window_copies(far):
                copy.wait_recv()

    def attend_head(head):
        cols = pl.ds(pl.multiple_of(head * HEAD_DIM, HEAD_DIM), HEAD_DIM)
        scores = lax.dot_general(
            win_k[:, cols], q_ref[:, cols], (((1,), (1,)), ((), ())),
            preferred_element_type=jnp.float32,
        )
        scores = scores * SCALE2 + mask[...]
        exponent = jnp.exp2(scores - jnp.max(scores, axis=0, keepdims=True))
        total = jnp.sum(exponent, axis=0, keepdims=True)
        blended = lax.dot_general(
            win_v[:, cols], exponent.astype(jnp.bfloat16), (((0,), (0,)), ((), ())),
            preferred_element_type=jnp.float32,
        )
        att[:, cols] = (blended / total).T.astype(jnp.bfloat16)

    per_step = HEADS // 4

    def second_step(step, carry):
        forward(second_group, step)
        for k in range(per_step):
            attend_head(step * per_step + k)
        return carry

    lax.fori_loop(0, 4, second_step, 0)

    width = stream.shape[1]
    squares = jnp.zeros((rows, 1), jnp.float32)
    for col in range(0, width, 512):
        cols = slice(col, col + 512)
        value = x_ref[:, cols].astype(jnp.float32) + jnp.dot(
            att[...], all_o[:, cols], preferred_element_type=jnp.float32
        )
        stream[:, cols] = value
        squares = squares + jnp.sum(value * value, axis=1, keepdims=True)
    inverse = lax.rsqrt(squares / width + 1e-05)
    normed[...] = (stream[...] * inverse * gain_ref[...]).astype(jnp.bfloat16)

    def last_step(step, carry):
        forward(second_group, step)
        return carry

    lax.fori_loop(4, steps[0] - 2, last_step, 0)
    finish(second_group)

    def near_copies(i, near, way):
        there = pl.ds((1 - way) * 2 * rows, rows)
        there = pl.ds(0, rows) if way == 0 else pl.ds(2 * rows, rows)
        target = (me + 1) % n if way == 0 else (me + n - 1) % n
        return send(
            near.at[pl.ds(rows, rows)], near.at[there], (near_send, near_recv), 2 * i + way, target
        )

    for i, (near, weight) in enumerate(((near_k, all_k), (near_v, all_v))):
        for col in range(0, near.shape[1], 512):
            cols = slice(col, col + 512)
            near[pl.ds(rows, rows), cols] = jnp.dot(
                normed[...], weight[:, cols], preferred_element_type=jnp.float32
            ).astype(jnp.bfloat16)

        @pl.when(me < n - 1)
        def _():
            near_copies(i, near, 0).start()

        @pl.when(me >= 1)
        def _():
            near_copies(i, near, 1).start()

        @pl.when(me == 0)
        def _():
            near[pl.ds(0, rows), :] = jnp.zeros((rows, near.shape[1]), jnp.bfloat16)

        @pl.when(me == n - 1)
        def _():
            near[pl.ds(2 * rows, rows), :] = jnp.zeros((rows, near.shape[1]), jnp.bfloat16)

    counted = lax.broadcasted_iota(jnp.int32, all_c.shape, 0)
    taken = (counted % 8 == 0) & (counted // 8 < me)
    earlier = jnp.sum(jnp.where(taken, all_c[...], 0), axis=0, keepdims=True)
    start_ref[...] = jnp.broadcast_to(earlier, start_ref.shape)

    def sent(step, carry):
        for piece in range(len(pieces)):
            for way in (0, 1):
                ring(piece, way, step).wait_send()
        return carry

    lax.fori_loop(0, steps[1], sent, 0)
    for piece in range(len(pieces)):
        ring(piece, 0, steps[0] - 1).wait_send()
    for far in range(1, reach + 1):
        @pl.when(me + far < n)
        def _():
            for copy in window_copies(far):
                copy.wait_send()
    for i, near in enumerate((near_k, near_v)):
        @pl.when(me < n - 1)
        def _():
            near_copies(i, near, 0).wait_send()
            near_copies(i, near, 1).wait_recv()

        @pl.when(me >= 1)
        def _():
            near_copies(i, near, 1).wait_send()
            near_copies(i, near, 0).wait_recv()


def semantic_part(n, queries, keys, values, inputs, gain, out_proj, key_proj, value_proj, counts):
    rows, width = queries.shape
    model = inputs.shape[1]
    reach = (W - 1 + rows - 1) // rows
    bf16, f32 = jnp.bfloat16, jnp.float32
    window = (reach + 1) * rows
    ring_sems = 5 * 2 * (n // 2)
    vmem = pl.BlockSpec(memory_space=pltpu.VMEM)
    dma = pltpu.SemaphoreType.DMA
    return pl.pallas_call(
        functools.partial(semantic_kernel, n),
        in_specs=[vmem] * 9,
        out_specs=[vmem] * 3,
        out_shape=[
            jax.ShapeDtypeStruct((3 * rows, width), bf16),
            jax.ShapeDtypeStruct((3 * rows, width), bf16),
            jax.ShapeDtypeStruct((8, 128), jnp.int32),
        ],
        scratch_shapes=[
            pltpu.VMEM((window, width), bf16),
            pltpu.VMEM((window, width), bf16),
            pltpu.VMEM((n * out_proj.shape[0], model), bf16),
            pltpu.VMEM((n * key_proj.shape[0], width), bf16),
            pltpu.VMEM((n * value_proj.shape[0], width), bf16),
            pltpu.VMEM((n * 8, 128), jnp.int32),
            pltpu.VMEM((rows, width), bf16),
            pltpu.VMEM((rows, model), f32),
            pltpu.VMEM((rows, model), bf16),
            pltpu.VMEM((window, rows), f32),
            dma((ring_sems,)), dma((ring_sems,)),
            dma((2 * reach,)), dma((2 * reach,)),
            dma((4,)), dma((4,)),
        ],
        compiler_params=pltpu.CompilerParams(
            collective_id=0, has_side_effects=True, vmem_limit_bytes=48 * 1024 * 1024
        ),
        cost_estimate=pl.CostEstimate(
            flops=2 * rows * width * (2 * window + 3 * model), bytes_accessed=8 * 1024 * 1024,
            transcendentals=rows * window * HEADS,
        ),
        name="semantic_part",
    )(queries, keys, values, inputs, gain, out_proj, key_proj, value_proj, counts)


def on_device(
    n, sem_queries, sem_keys, sem_values, sem_inputs, out_proj, norm_gain, key_proj, value_proj,
    slopes, coarse_queries, counts, band_bounds,
):
    near_keys, near_values, start = semantic_part(
        n, sem_queries, sem_keys, sem_values, sem_inputs, norm_gain[None, :], out_proj, key_proj,
        value_proj, jnp.broadcast_to(counts[:, None], (8, 128)),
    )
    return cross_attention(
        band_bounds, start, counts, slopes, coarse_queries, near_keys, near_values
    )


def solution(mesh):
    return jax.shard_map(
        functools.partial(on_device, mesh.shape["ctx"]),
        mesh=mesh,
        in_specs=(
            P(("groups", "ctx"), None),
            P(("groups", "ctx"), None),
            P(("groups", "ctx"), None),
            P(("groups", "ctx"), None),
            P("ctx", None),
            P(),
            P("ctx", None),
            P("ctx", None),
            P(),
            P(("groups", "ctx"), None),
            P(("groups", "ctx")),
            P(("groups", "ctx"), None),
        ),
        out_specs=P(("groups", "ctx"), None),
        check_vma=False,
    )
```

time: 264 us -> 161 us (0.61)
  the two profiles are of different devices: /device:TPU:0 before, /device:TPU:9 now
where the time goes in v2:
time: 161 us; the launch traced here: 160 us
  Pallas kernels  149 us (93%)
  local copies, waits for them, and re-layouts  10.1 us (6%)
    pallas_call x1, Pallas kernels, semantic_part(): pl.pallas_call(functools.partial(semantic_kernel, n), in_specs=[vmem] * 9...  132 us
    pallas_call x1, Pallas kernels, cross_attention(): pl.pallas_call(cross_kernel, grid=(blocks,), in_specs=[smem, smem, smem,...  16.9 us
    unnamed x23, local copies, waits for them, and re-layouts  10.1 us

profile of v2, /device:TPU:9, one launch (start us, length us, event | category | flops | bytes accessed | tf_op | source)
XLA Modules:
  0.0 159.6 jit_solution(9881225354189129148)
XLA Ops:
  0.7 0.8 copy.13.bounds
  1.4 0.0 copy-start.1
  1.4 1.2 copy-done.1
  2.6 0.0 copy-start.2
  2.6 1.0 copy-done.2
  3.7 0.0 copy-start.3
  3.7 1.0 copy-done.3
  4.7 0.0 copy-start.4
  4.7 1.0 copy-done.4
  5.8 0.0 copy-start.5
  5.8 0.9 copy-done.5
  6.7 0.0 copy-start.6
  6.7 0.9 copy-done.6
  7.7 0.0 copy-start.7
  7.7 0.9 copy-done.7
  8.6 0.0 copy-start.8
  8.6 0.7 copy-done.8
  9.3 0.0 copy-start
  9.3 0.0 copy-start.9
  9.3 132.0 %semantic_part.1 = (bf16[768,1024]{1,0:T(8,128)(2,1)S(1)}, bf16[768,1024]{1,0:T(8,128)(2,1)}, s32[8,128]{1,0:T(8,128)S(1)}) custom-call(bf16[256,1024]{1,0:T(8,128)(2,1)S(1)} %copy-done.2, bf16[256,1024]{1,0:T(8,128)(2,1)S(1)} %copy-done.3, bf16[256,1024]{1,0:T(8,128)(2,1)S(1)} %copy-done.4, bf16[256,2048]{1,0:T(8,128)(2,1)S(1)} %copy-done.1, ...), custom_call_target="tpu_custom_call" | custom-call | flops 4026531840 | bytes 8388608 | tf_op jit(solution)/shard_map/semantic_part/pallas_call | solution.py:319
  141.3 0.0 copy-done
  141.4 0.0 copy-done.9
  141.4 0.0 copy-start.10
  141.4 1.4 copy-done.10
  142.8 16.9 %cross_attention.1 = bf16[1024,1024]{1,0:T(8,128)(2,1)} custom-call(s32[4,2]{1,0:T(4,128)S(1)} %copy.13.bounds, s32[8,128]{1,0:T(8,128)S(1)} %get-tuple-element.8.start, s32[1]{0:T(128)} %copy.14.counts, f32[8]{0:T(128)S(1)} %copy-done.9, bf16[1024,1024]{1,0:T(8,128)(2,1)S(1)} %copy-done, bf16[768,1024]{1,0:T(8,128)(2,1)S(1)} %get-tuple-element.9.k_ref, ...), custom_call_target="tpu_custom_call" | custom-call | flops 2214592512 | bytes 8388608 | tf_op jit(solution)/shard_map/cross_attention/pallas_call | solution.py:60
  (1 shorter events, 0.0 us)
Async XLA Ops:
  1.4 1.2 copy-start.1
  2.6 1.0 copy-start.2
  3.7 1.0 copy-start.3
  4.7 1.0 copy-start.4
  5.8 0.9 copy-start.5
  6.7 0.9 copy-start.6
  7.7 0.9 copy-start.7
  8.6 0.7 copy-start.8
  9.3 132.0 %copy-start = (bf16[1024,1024]{1,0:T(8,128)(2,1)S(1)}, bf16[1024,1024]{1,0:T(8,128)(2,1)}, u32[]{:S(2)}) copy-start(bf16[1024,1024]{1,0:T(8,128)(2,1)} %q_ref.3) | copy-start | bytes 6291460
  9.3 132.0 %copy-start.9 = (f32[8]{0:T(128)S(1)}, f32[8]{0:T(128)}, u32[]{:S(2)}) copy-start(f32[8]{0:T(128)} %slopes.1) | copy-start | bytes 100
  141.4 1.4 copy-start.10
